TPU v7x, 512 devices: a whole 4x4x16 slice. The times are simulated.
512 devices in a mesh: grp: 4 (over y), resp: 16 (over z_lo, core), tp: 8 (over z_hi, x).
Axes of the slice: x: 4, y: 4, z: 16 (z_hi: 2, z_lo: 8; z = z_hi * 8 + z_lo), core: 2. Of those that a mesh axis runs over, the one named last changes fastest.
Arguments:
- queries: bfloat16 [8192, 64, 576], P(('grp', 'resp'), 'tp'), parts along dimension 0, may hold values from -44 to 44
- grad_out: bfloat16 [8192, 64, 512], P(('grp', 'resp'), 'tp'), parts along dimension 0, may hold values from -32 to 32
- prompt_kv: bfloat16 [3072, 576], P(('grp', 'resp')), parts along dimension 0, may hold values from -5 to 5
- resp_kv: bfloat16 [8192, 576], P(('grp', 'resp')), parts along dimension 0, may hold values from -6 to 6
- lengths: int32 [64], P(('grp', 'resp')), parts along dimension 0, may hold values from 16 to 128, as said below
Outputs:
- grad_queries: bfloat16 [8192, 64, 576], P(('grp', 'resp'), 'tp'), parts along dimension 0
- grad_prompt: bfloat16 [3072, 576], P(('grp', 'resp')), parts along dimension 0
- grad_resp: bfloat16 [8192, 576], P(('grp', 'resp')), parts along dimension 0
There are 4 independent parts, one for each index of `grp`. A program takes and returns all parts, laid end to end along the dimension named above; each array names one. Nothing has to cross between parts.
Inputs may be any that keep to these rules, and one draw needn't show every extreme that they name: `lengths`: every response has length 16 or more, and some response has length 128.
All inputs are finite; a program needn't handle non-finite values.
Results may differ from a plain program's by a relative error of at most 0.012.
Values may be sent and summed in bfloat16 or wider, within the bound.
No kernel may reach another device: no remote copies, remote signals or barrier semaphores. Data moves between devices by JAX's collectives and lax.ppermute only.
A program may use at most 64 MiB of HBM per device.

v0:
```python
import jax
import jax.numpy as jnp
from jax import lax
from jax.sharding import PartitionSpec as P

softmax_scale = 192 ** (-0.5)
masked_value = -1e30


def local_grads(queries, grad_out, prompt_all, resp_kv, length):
    rows, heads, width = queries.shape
    latent = grad_out.shape[2]
    prompt_rows = prompt_all.shape[0]
    keys = jnp.concatenate([prompt_all, resp_kv], 0)
    total = keys.shape[0]
    position = jnp.arange(rows, dtype=jnp.int32)
    key_pos = jnp.arange(total, dtype=jnp.int32) - prompt_rows
    allowed = key_pos[None, :] <= position[:, None]
    live = position < length
    q_flat = queries.reshape(rows * heads, width)
    scores = (
        jnp.dot(q_flat, keys.T, preferred_element_type=jnp.float32).reshape(rows, heads, total)
        * softmax_scale
    )
    scores = jnp.where(allowed[:, None, :], scores, masked_value)
    top = jnp.max(scores, axis=-1, keepdims=True)
    expo = jnp.exp(scores - top)
    probs = (expo / jnp.sum(expo, axis=-1, keepdims=True)).reshape(rows * heads, total)
    probs_b = probs.astype(jnp.bfloat16)
    d_flat = jnp.where(live[:, None, None], grad_out, jnp.zeros_like(grad_out)).reshape(
        rows * heads, latent
    )
    values = keys[:, :latent]
    out_vals = jnp.dot(probs_b, values, preferred_element_type=jnp.float32)
    delta = jnp.sum(d_flat.astype(jnp.float32) * out_vals, axis=-1, keepdims=True)
    d_prob = jnp.dot(d_flat, values.T, preferred_element_type=jnp.float32)
    d_score = (softmax_scale * probs * (d_prob - delta)).astype(jnp.bfloat16)
    d_query = (
        jnp.dot(d_score, keys, preferred_element_type=jnp.float32)
        .astype(jnp.bfloat16)
        .reshape(rows, heads, width)
    )
    dims = (((0,), (0,)), ((), ()))
    d_keys = lax.dot_general(d_score, q_flat, dims, preferred_element_type=jnp.float32)
    d_vals = lax.dot_general(probs_b, d_flat, dims, preferred_element_type=jnp.float32)
    d_kv = jnp.concatenate([d_keys[:, :latent] + d_vals, d_keys[:, latent:]], 1)
    return (d_query, d_kv[:prompt_rows], d_kv[prompt_rows:])


def body(queries, grad_out, prompt_kv, resp_kv, lengths):
    prompt_all = lax.all_gather(prompt_kv, "resp", axis=0, tiled=True)
    d_query, prompt_term, resp_term = local_grads(
        queries, grad_out, prompt_all, resp_kv, lengths[0]
    )
    mine = lax.psum_scatter(prompt_term, "resp", scatter_dimension=0, tiled=True)
    prompt_sum, resp_sum = lax.psum((mine, resp_term), "tp")
    grad_prompt = prompt_sum.astype(jnp.bfloat16)
    return (d_query, grad_prompt, resp_sum.astype(jnp.bfloat16))


def solution(mesh):
    return jax.shard_map(
        body,
        mesh=mesh,
        in_specs=(
            P(("grp", "resp"), "tp", None),
            P(("grp", "resp"), "tp", None),
            P(("grp", "resp"), None),
            P(("grp", "resp"), None),
            P(("grp", "resp")),
        ),
        out_specs=(
            P(("grp", "resp"), "tp", None),
            P(("grp", "resp"), None),
            P(("grp", "resp"), None),
        ),
        check_vma=False,
    )
```

profile of v0, /device:TPU:480, one launch (start us, length us, event | category | flops | bytes accessed | tf_op | source)
XLA Modules:
  0.0 270.5 jit_solution(6868184996795718049)
XLA Ops:
  7.2 0.0 copy-start.4
  7.2 0.0 reduce-scatter.4.cloned.1.call-start
  7.9 0.1 iota_compare_fusion
  8.0 0.0 copy-start
  8.0 1.1 copy.21
  9.1 0.4 broadcast_bitcast_fusion
  9.6 2.0 copy.23
  11.5 0.0 copy-done.4
  11.5 29.9 %all_gather.3 = bf16[768,576]{1,0:T(8,128)(2,1)} all-gather(bf16[48,576]{1,0:T(8,128)(2,1)S(1)} %copy-done.4), channel_id=1, replica_groups=mesh['grp'=4,'resp'=16,'tp'=8] {'resp'}, dimensions={0}, use_global_device_ids=true | all-gather | bytes 940032 | tf_op jit(solution)/shard_map/all_gather | solution.py:51
  41.4 0.0 copy-done
  41.4 0.2 select_bitcast_fusion
  41.6 1.3 copy.24
  43.0 2.2 copy.22
  45.2 3.2 %fusion.13 = (f32[1024]{0:T(1024)S(1)}, f32[1024,896]{0,1:T(8,128)S(1)}) fusion(pred[1024,896]{0,1:T(32,128)(4,1)} %copy.23, bf16[128,8,576]{2,1,0:T(8,128)(2,1)S(1)} %copy.22, bf16[128,576]{1,0:T(8,128)(2,1)S(1)} %copy.21, bf16[768,576]{1,0:T(8,128)(2,1)} %all_gather.3), kind=kOutput, calls=%fused_computation.27 | convolution fusion | flops 1061780480 | bytes 6803456 | tf_op jit(solution)/shard_map/dot_general | solution.py:22
  48.4 0.0 copy-start.1
  48.4 0.0 copy-start.2
  48.4 0.5 fusion.1
  49.0 0.7 copy-done.1
  49.6 0.3 copy-done.2
  49.9 1.4 multiply_reduce_fusion
  51.3 1.4 multiply_convert_fusion
  52.7 0.0 copy-start.5
  52.7 1.5 fusion.3
  54.2 0.0 copy-done.5
  54.2 1.4 slice_add_fusion
  55.6 1.4 fusion.2
  57.0 0.0 copy-start.3
  57.0 2.9 %copy.30 = f32[768,576]{1,0:T(8,128)} copy(f32[768,576]{0,1:T(8,128)} %fusion.2) | data formatting | bytes 3538944
  59.9 0.0 reduce-scatter.4.cloned.1.call-update
  59.9 0.0 copy-done.3
  59.9 3.9 %convolution_convert_fusion = bf16[1024,576]{0,1:T(8,128)(2,1)} fusion(bf16[1024,896]{0,1:T(8,128)(2,1)} %copy-done.5, bf16[128,576]{1,0:T(8,128)(2,1)S(1)} %copy.21, bf16[768,576]{1,0:T(8,128)(2,1)S(1)} %copy-done.3), kind=kOutput, calls=%fused_computation.11 | convolution fusion | flops 1059618816 | bytes 4046848 | tf_op jit(solution)/shard_map/dot_general | solution.py:39
  63.9 1.7 copy.26
  65.6 1.8 copy.27
  67.4 96.0 %reduce-scatter.4.cloned.1.call-done = f32[48,576]{1,0:T(8,128)} async-done(((f32[768,576]{1,0:T(8,128)}), f32[48,576]{1,0:T(8,128)}) %reduce-scatter.4.cloned.1.call-update) | async-done | bytes 110608
  163.4 1.0 copy.31
  164.5 98.4 %all-reduce.2 = (bf16[48,576]{0,1:T(8,128)(2,1)S(1)}, bf16[128,576]{0,1:T(8,128)(2,1)}) all-reduce(f32[48,576]{0,1:T(8,128)S(1)} %copy.31, f32[128,576]{0,1:T(8,128)S(1)} %pad_maximum_fusion.6), channel_id=1, replica_groups=mesh['grp'=4,'resp'=16,'tp'=8] {'tp'}, use_global_device_ids=true, to_apply=%region_4.5 | all-reduce | flops 101376 | bytes 608256 | tf_op jit(solution)/shard_map/psum | solution.py:56
  262.9 0.7 copy.28
  (4 shorter events, 0.0 us)
Async XLA Ops:
  7.2 4.4 %copy-start.4 = (bf16[48,576]{1,0:T(8,128)(2,1)S(1)}, bf16[48,576]{1,0:T(8,128)(2,1)}, u32[]{:S(2)}) copy-start(bf16[48,576]{1,0:T(8,128)(2,1)} %param.7) | copy-start | bytes 165892
  7.2 156.2 %reduce-scatter.4.cloned.1.call-start = ((), (), s32[]{:S(2)}) async-start(), calls=%async_computation.1 | async-start | bytes 2088960
  8.0 33.5 %copy-start = (bf16[128,8,512]{2,1,0:T(8,128)(2,1)S(1)}, bf16[128,8,512]{2,1,0:T(8,128)(2,1)}, u32[]{:S(2)}) copy-start(bf16[128,8,512]{2,1,0:T(8,128)(2,1)} %param.6) | copy-start | bytes 3145732
  48.4 1.2 copy-start.1
  48.4 1.5 copy-start.2
  52.7 1.5 copy-start.5
  57.0 2.9 %copy-start.3 = (bf16[768,576]{1,0:T(8,128)(2,1)S(1)}, bf16[768,576]{1,0:T(8,128)(2,1)}, u32[]{:S(2)}) copy-start(bf16[768,576]{1,0:T(8,128)(2,1)} %all_gather.3) | copy-start | bytes 2654212
Sparse Core Ops, SparseCore 0:
  60.0 103.3 reduce-scatter.3
where the time goes:
time: 271 us; the launch traced here: 270 us
  blocking collectives  128 us (47%)
  waiting for transfers between devices  96.1 us (35%)
  local copies, waits for them, and re-layouts  16.2 us (6%)
  between operations  14.8 us (5%)
  matrix products  12.8 us (5%)
    psum x1, blocking collectives, body(): prompt_sum, resp_sum = lax.psum((mine, resp_term), 'tp')  98.4 us
    unnamed x2, waiting for transfers between devices  96.1 us
    all_gather x1, blocking collectives, body(): prompt_all = lax.all_gather(prompt_kv, 'resp', axis=0, tiled=True)  29.9 us
    unnamed x18, local copies, waits for them, and re-layouts  10.8 us
  transfers between devices with their start and end apart: 1, of which 1 were waited for; matrix products, arithmetic and copies ran while one was open for 3% of the time, Pallas kernels for 0%

commit v1 on v0

--- a/solution.py
+++ b/solution.py
@@ -5,6 +5,9 @@
 
 softmax_scale = 192 ** (-0.5)
 masked_value = -1e30
+lay_the_scales = lambda message: jnp.concatenate(
+    lax.all_to_all(jnp.stack([message] * lax.axis_size("resp"), axis=0), "resp", 0, 0), axis=0
+)
 
 
 def local_grads(queries, grad_out, prompt_all, resp_kv, length):
@@ -48,7 +51,7 @@
 
 
 def body(queries, grad_out, prompt_kv, resp_kv, lengths):
-    prompt_all = lax.all_gather(prompt_kv, "resp", axis=0, tiled=True)
+    prompt_all = lay_the_scales(prompt_kv)
     d_query, prompt_term, resp_term = local_grads(
         queries, grad_out, prompt_all, resp_kv, lengths[0]
     )

time: 271 us -> 283 us (1.044)
  the two profiles are of different devices: /device:TPU:480 before, /device:TPU:24 now
where the time goes in v1:
time: 283 us; the launch traced here: 282 us
  waiting for transfers between devices  137 us (48%)
  blocking collectives  83.5 us (30%)
  local copies, waits for them, and re-layouts  16.9 us (6%)
  matrix products  15.3 us (5%)
  between operations  14.9 us (5%)
  starting transfers between devices  12.7 us (4%)
    unnamed x2, waiting for transfers between devices  102 us
    psum x1, blocking collectives, body(): prompt_sum, resp_sum = lax.psum((mine, resp_term), 'tp')  83.5 us
    all_to_all x1, waiting for transfers between devices, lax.all_to_all(jnp.stack([message] * lax.axis_size('resp'), axis=0), 'res...  34.5 us
    all_to_all x1, starting transfers between devices, lax.all_to_all(jnp.stack([message] * lax.axis_size('resp'), axis=0), 'res...  12.7 us
    unnamed x14, local copies, waits for them, and re-layouts  9.46 us
  transfers between devices with their start and end apart: 2, of which 2 were waited for; matrix products, arithmetic and copies ran while one was open for 5% of the time, Pallas kernels for 0%

profile of v1, /device:TPU:24, one launch (start us, length us, event | category | flops | bytes accessed | tf_op | source)
XLA Modules:
  0.0 282.3 jit_solution(653064335418278265)
XLA Ops:
  7.2 0.0 copy-start.2
  7.2 1.9 stack.2
  9.1 12.7 %all-to-all-start = ((bf16[16,48,576]{2,1,0:T(8,128)(2,1)}), bf16[16,48,576]{2,1,0:T(8,128)(2,1)}, u32[]{:S(2)}, u32[]{:S(2)}) async-start(bf16[16,48,576]{2,1,0:T(8,128)(2,1)} %stack.2), calls=%async_computation | async-start | bytes 1966080 | tf_op jit(solution)/shard_map/all_to_all | solution.py:9
  21.8 0.0 copy-start
  21.8 0.0 reduce-scatter.4.cloned.1.call-start
  22.5 0.0 copy-done.2
  22.5 0.2 copy.21
  22.7 0.1 iota_compare_fusion
  22.8 0.4 broadcast_bitcast_fusion
  23.2 2.0 copy.23
  25.2 0.0 copy-done
  25.2 0.2 select_bitcast_fusion
  25.4 1.5 copy.24
  26.9 2.2 copy.22
  29.1 34.5 %all-to-all-done = bf16[16,48,576]{2,1,0:T(8,128)(2,1)} async-done(((bf16[16,48,576]{2,1,0:T(8,128)(2,1)}), bf16[16,48,576]{2,1,0:T(8,128)(2,1)}, u32[]{:S(2)}, u32[]{:S(2)}) %all-to-all-start) | async-done | bytes 884768 | tf_op jit(solution)/shard_map/all_to_all | solution.py:9
  63.6 3.2 %fusion.13 = (f32[1024]{0:T(1024)S(1)}, f32[1024,896]{0,1:T(8,128)S(1)}) fusion(pred[1024,896]{0,1:T(32,128)(4,1)} %copy.23, bf16[128,8,576]{2,1,0:T(8,128)(2,1)S(1)} %copy.22, bf16[128,576]{1,0:T(8,128)(2,1)S(1)} %copy.21, bf16[768,576]{1,0:T(8,128)(2,1)} %bitcast.1), kind=kOutput, calls=%fused_computation.27 | convolution fusion | flops 1061780480 | bytes 6803456 | tf_op jit(solution)/shard_map/dot_general | solution.py:25
  66.8 0.0 copy-start.1
  66.8 0.5 fusion.1
  67.4 0.7 copy-done.1
  68.1 2.5 multiply_reduce_fusion
  70.6 2.5 multiply_convert_fusion
  73.1 0.0 copy-start.3
  73.1 1.5 fusion.3
  74.6 0.0 copy-done.3
  74.6 1.4 slice_add_fusion
  76.0 1.4 fusion.2
  77.4 2.8 %copy.30 = f32[768,576]{1,0:T(8,128)} copy(f32[768,576]{0,1:T(8,128)} %fusion.2) | data formatting | bytes 3538944
  80.2 0.0 reduce-scatter.4.cloned.1.call-update
  80.2 4.2 %convolution_convert_fusion = bf16[1024,576]{0,1:T(8,128)(2,1)} fusion(bf16[1024,896]{0,1:T(8,128)(2,1)} %copy-done.3, bf16[128,576]{1,0:T(8,128)(2,1)S(1)} %copy.21, bf16[768,576]{1,0:T(8,128)(2,1)} %bitcast.1), kind=kOutput, calls=%fused_computation.11 | convolution fusion | flops 1059618816 | bytes 4046848 | tf_op jit(solution)/shard_map/dot_general | solution.py:42
  84.4 1.7 copy.26
  86.1 1.8 copy.27
  87.9 102.2 %reduce-scatter.4.cloned.1.call-done = f32[48,576]{1,0:T(8,128)} async-done(((f32[768,576]{1,0:T(8,128)}), f32[48,576]{1,0:T(8,128)}) %reduce-scatter.4.cloned.1.call-update) | async-done | bytes 110608
  190.1 1.0 copy.31
  191.1 83.5 %all-reduce.2 = (bf16[48,576]{0,1:T(8,128)(2,1)S(1)}, bf16[128,576]{0,1:T(8,128)(2,1)}) all-reduce(f32[48,576]{0,1:T(8,128)S(1)} %copy.31, f32[128,576]{0,1:T(8,128)S(1)} %pad_maximum_fusion.6), channel_id=1, replica_groups=mesh['grp'=4,'resp'=16,'tp'=8] {'tp'}, use_global_device_ids=true, to_apply=%region_4.5 | all-reduce | flops 101376 | bytes 608256 | tf_op jit(solution)/shard_map/psum | solution.py:59
  274.7 0.7 copy.28
  (4 shorter events, 0.0 us)
Async XLA Ops:
  7.2 15.4 %copy-start.2 = (bf16[128,576]{0,1:T(8,128)(2,1)S(1)}, bf16[128,576]{0,1:T(8,128)(2,1)}, u32[]{:S(2)}) copy-start(bf16[128,576]{0,1:T(8,128)(2,1)} %param.8) | copy-start | bytes 442372
  9.1 54.5 %all-to-all-start = ((bf16[16,48,576]{2,1,0:T(8,128)(2,1)}), bf16[16,48,576]{2,1,0:T(8,128)(2,1)}, u32[]{:S(2)}, u32[]{:S(2)}) async-start(bf16[16,48,576]{2,1,0:T(8,128)(2,1)} %stack.2), calls=%async_computation | async-start | bytes 1966080 | tf_op jit(solution)/shard_map/all_to_all | solution.py:9
  21.8 3.5 %copy-start = (bf16[128,8,512]{2,1,0:T(8,128)(2,1)S(1)}, bf16[128,8,512]{2,1,0:T(8,128)(2,1)}, u32[]{:S(2)}) copy-start(bf16[128,8,512]{2,1,0:T(8,128)(2,1)} %param.6) | copy-start | bytes 3145732
  21.8 168.3 %reduce-scatter.4.cloned.1.call-start = ((), (), s32[]{:S(2)}) async-start(), calls=%async_computation.2 | async-start | bytes 2088960
  66.8 1.2 copy-start.1
  73.1 1.5 copy-start.3
Sparse Core Ops, SparseCore 0:
  80.3 109.7 reduce-scatter.3
